TPU v7x, 512 devices: a whole 4x8x8 slice. The times are simulated.
512 devices in a mesh: grp: 16 (over y_hi, x, core), dev: 32 (over z, y_lo).
Axes of the slice: x: 4, y: 8 (y_hi: 2, y_lo: 4; y = y_hi * 4 + y_lo), z: 8, core: 2. Of those that a mesh axis runs over, the one named last changes fastest.
Arguments:
- spectra: float32 [2048, 2, 2, 2048], P(('grp', 'dev')), may hold values from -120 to 120
- counts: int32 [2, 512], replicated, may hold values from 0 to 4
Outputs:
- correlations: bfloat16 [2, 2048, 128, 128], P(None, ('grp', 'dev'))
Inputs may be any that keep to these rules, and one draw needn't show every extreme that they name: counts[s, b] live channels are the first ones of block b in segment s.
All inputs are finite; a program needn't handle non-finite values.
Results may differ from a plain program's by a relative error of at most 0.007.
Values may be sent and summed in bfloat16 or wider, within the bound.
A program may use at most 64 MiB of HBM per device.

v0:
```python
import math

import jax
import jax.numpy as jnp
from jax import lax
from jax.sharding import PartitionSpec as P

LAGS = 128
ROUNDS = 2


def from_behind(block, axis, distance):
    devices = range(lax.axis_size(axis))
    route = [((i - distance) % len(devices), i) for i in devices]
    return lax.ppermute(block, axis, route)


def valid_rows(counts, first_row, row_count, block_width):
    row_ids = first_row + jnp.arange(row_count, dtype=jnp.int32)
    block_ids = row_ids // block_width
    inside = row_ids - block_ids * block_width
    block_range = jnp.arange(counts.shape[1], dtype=jnp.int32)
    matches = block_ids[:, None] == block_range[None, :]
    row_counts = jnp.sum(
        jnp.where(matches[:, :, None], jnp.transpose(counts)[None, :, :], 0), axis=1
    )
    return (inside[:, None] < row_counts).astype(jnp.float32)


def lag_table(bins_count, lags_count):
    frequency = jnp.arange(bins_count, dtype=jnp.int32)
    lag_index = jnp.arange(lags_count, dtype=jnp.int32) - lags_count // 2
    angles = jnp.mod(frequency[:, None] * lag_index[None, :], 2 * bins_count).astype(
        jnp.float32
    ) * (math.pi / bins_count)
    table = jnp.concatenate([jnp.cos(angles), -jnp.sin(angles)], 0) / math.sqrt(bins_count)
    return table.astype(jnp.bfloat16)


def whiten(spectra, live):
    energy = jnp.mean(spectra * spectra, axis=(2, 3))
    return (spectra * (live / jnp.sqrt(energy + 1e-06))[:, :, None, None]).astype(jnp.bfloat16)


def pair_slab(left_block, live_left, right_block, live_right, table):
    swapped = jnp.stack([-right_block[:, :, 1], right_block[:, :, 0]], 2)
    real_part = jnp.einsum(
        "iscf,jscf->ijf", left_block, right_block, preferred_element_type=jnp.float32
    )
    imag_part = jnp.einsum(
        "iscf,jscf->ijf", left_block, swapped, preferred_element_type=jnp.float32
    )
    intersection = jnp.dot(live_left, jnp.transpose(live_right), precision=lax.Precision.HIGHEST)
    inverse = 1.0 / jnp.maximum(intersection, 1.0)
    stacked = (jnp.concatenate([real_part, imag_part], -1) * inverse[:, :, None]).astype(
        jnp.bfloat16
    )
    left_rows = left_block.shape[0]
    right_rows = right_block.shape[0]
    lagged = jnp.dot(
        stacked.reshape(left_rows * right_rows, -1), table, preferred_element_type=jnp.float32
    )
    return lagged.astype(jnp.bfloat16).reshape(left_rows, right_rows, -1)


def slab_rows(row_count, block_width, other_rows):
    target = block_width * max(1, 512 // (block_width * other_rows))
    return math.gcd(row_count, target)


def local(spectra, counts):
    block_width = spectra.shape[0]
    device_count = lax.axis_size("dev")
    group_count = lax.axis_size("grp")
    group_rows = block_width * device_count
    group_index = lax.axis_index("grp")
    device_index = lax.axis_index("dev")
    mine_first = (group_index * device_count + device_index) * block_width
    mine_live = valid_rows(counts, mine_first, block_width, block_width)
    mine_white = whiten(spectra, mine_live)
    table = lag_table(spectra.shape[3], LAGS)
    stacked_rounds = []
    for offset in range(1, ROUNDS + 1):
        partner = from_behind(mine_white, "grp", offset)
        partner_first = jnp.mod(group_index - offset, group_count) * group_rows

        def crossing(incoming, first_row, partner_first=partner_first):
            row_count = incoming.shape[0]
            incoming_live = valid_rows(counts, partner_first, row_count, block_width)
            step_rows = slab_rows(row_count, block_width, block_width)

            def single_slab(position):
                return pair_slab(mine_white, mine_live, incoming, incoming_live, table)

            pieces = lax.map(single_slab, jnp.arange(row_count // step_rows, dtype=jnp.int32))
            return jnp.transpose(pieces, (1, 0, 2, 3)).reshape(block_width, row_count, -1)

        stacked_rounds.append(
            crossing(lax.all_gather(partner, "dev", axis=0, tiled=True), jnp.int32(0))
        )
    return jnp.stack(stacked_rounds, 0)


def solution(mesh):
    placed = (P(("grp", "dev"), None, None, None), P())
    return jax.shard_map(
        local,
        mesh=mesh,
        in_specs=placed,
        out_specs=P(None, ("grp", "dev"), None, None),
        check_vma=False,
    )
```

profile of v0, /device:TPU:6, one launch (start us, length us, event | category | flops | bytes accessed | tf_op | source)
XLA Modules:
  0.0 385.5 jit_solution(1181672086979482276)
XLA Ops:
  6.5 0.0 all-gather.3.cloned.1.call-start
  6.6 0.1 iota_compare_fusion.2
  6.6 1.1 multiply_reduce_fusion
  7.7 0.1 copy.23
  7.8 0.8 select_reduce_fusion.2
  8.6 1.0 fusion.26
  9.6 1.9 collective-permute-start
  11.6 3.7 collective-permute-done
  15.2 0.7 copy.25
  15.9 0.0 all-gather.3.cloned.1.call-update
  15.9 0.0 all-gather.5.cloned.1.call-start
  16.0 14.1 %collective-permute-start.1 = (bf16[4,2,2,2048]{3,0,2,1:T(4,128)(2,1)S(1)}, bf16[4,2,2,2048]{3,0,2,1:T(4,128)(2,1)S(1)}, u32[]{:S(2)}, u32[]{:S(2)}) collective-permute-start(bf16[4,2,2,2048]{3,0,2,1:T(4,128)(2,1)S(1)} %fusion.26), channel_id=1, source_target_pairs={{448,0},{480,32},{0,64},{32,96},{64,128},{96,160},{128,192},{160,2... | collective-permute-start | bytes 196616 | tf_op jit(solution)/shard_map/ppermute | solution.py:15
  30.1 1.9 collective-permute-done.1
  32.0 0.7 copy.31
  32.7 0.0 all-gather.5.cloned.1.call-update
  32.8 3.9 %copy.27 = bf16[4,2,2,2048]{0,1,2,3:T(2,128)(2,1)} copy(bf16[4,2,2,2048]{3,0,2,1:T(4,128)(2,1)S(1)} %fusion.26) | data formatting | bytes 131072 | tf_op jit(solution)/shard_map/convert_element_type | solution.py:42
  36.7 0.1 iota_compare_fusion
  36.8 0.1 iota_compare_fusion.1
  36.9 0.0 copy-done.6
  37.0 0.2 select_reduce_fusion.1
  37.1 0.2 fusion.18
  37.3 0.2 fusion.16
  37.5 5.3 %fusion.25 = (f32[2048,128]{1,0:T(8,128)S(1)}, f32[2048,128]{1,0:T(8,128)}) fusion(s32[128]{0:T(128)S(1)} %iota_add_fusion.1), kind=kLoop, calls=%fused_computation.37 | loop fusion | flops 3932160 | bytes 2097664 | tf_op jit(solution)/shard_map/cos | solution.py:36
  42.8 140.4 %all-gather.3.cloned.1.call-done = bf16[128,2,2,2048]{3,2,1,0:T(2,128)(2,1)} async-done(((bf16[4,2,2,2048]{3,2,1,0:T(2,128)(2,1)}), bf16[128,2,2,2048]{3,2,1,0:T(2,128)(2,1)}) %all-gather.3.cloned.1.call-update) | async-done | bytes 2097168 | tf_op jit(solution)/shard_map/all_gather | solution.py:99
  183.2 8.9 %copy.26 = bf16[128,2,2,2048]{0,1,2,3:T(2,128)(2,1)S(1)} copy(bf16[128,2,2,2048]{3,2,1,0:T(2,128)(2,1)} %all-gather.3.cloned.1.call-done) | data formatting | bytes 4194304 | tf_op jit(solution)/shard_map/all_gather | solution.py:99
  192.0 0.0 copy-start.1
  192.1 2.6 slice_negate_fusion.1
  194.7 0.0 copy-done.1
  194.7 6.6 %fusion.39 = f32[2048,128,4,1]{1,2,3,0:T(4,128)} fusion(bf16[128,2,2,2048]{0,1,2,3:T(2,128)(2,1)S(1)} %copy.26, bf16[4,2,2,2048]{0,1,2,3:T(2,128)(2,1)S(1)} %copy-done.1), kind=kOutput, calls=%fused_computation.78 | convolution fusion | flops 8388608 | bytes 6356992 | tf_op jit(solution)/shard_map/while/body/eval_jaxpr/iscf,jscf->ijf/dot_general | solution.py:47
  201.2 141.6 %all-gather.5.cloned.1.call-done = bf16[128,2,2,2048]{3,2,1,0:T(2,128)(2,1)} async-done(((bf16[4,2,2,2048]{3,2,1,0:T(2,128)(2,1)}), bf16[128,2,2,2048]{3,2,1,0:T(2,128)(2,1)}) %all-gather.5.cloned.1.call-update) | async-done | bytes 2097168 | tf_op jit(solution)/shard_map/all_gather | solution.py:99
  342.8 8.9 %copy.32 = bf16[128,2,2,2048]{0,1,2,3:T(2,128)(2,1)S(1)} copy(bf16[128,2,2,2048]{3,2,1,0:T(2,128)(2,1)} %all-gather.5.cloned.1.call-done) | data formatting | bytes 4194304 | tf_op jit(solution)/shard_map/all_gather | solution.py:99
  351.7 0.0 copy-start.2
  351.7 1.6 slice_negate_fusion
  353.3 0.0 copy-done.2
  353.3 0.0 copy-start.4
  353.4 5.3 %fusion.40 = f32[2048,128,4,1]{1,2,3,0:T(4,128)S(1)} fusion(bf16[128,2,2,2048]{0,1,2,3:T(2,128)(2,1)S(1)} %copy.32, bf16[4,2,2,2048]{0,1,2,3:T(2,128)(2,1)S(1)} %copy-done.2), kind=kOutput, calls=%fused_computation.79 | convolution fusion | flops 8388608 | bytes 6356992 | tf_op jit(solution)/shard_map/while/body/eval_jaxpr/iscf,jscf->ijf/dot_general | solution.py:47
  358.7 6.0 %fusion.8 = f32[2048,128,4,1]{1,2,3,0:T(4,128)S(1)} fusion(bf16[4,2,2,2048]{0,1,2,3:T(2,128)(2,1)S(1)} %copy-done.2, bf16[128,2,1,2048]{0,1,2,3:T(2,128)(2,1)S(1)} %copy-done.5, bf16[128,2,1,2048]{0,1,2,3:T(2,128)(2,1)S(1)} %copy-done.4), kind=kOutput, calls=%fused_computation.15 | convolution fusion | flops 12582912 | bytes 6356992 | tf_op jit(solution)/shard_map/while/body/eval_jaxpr/iscf,jscf->ijf/dot_general | solution.py:50
  364.7 0.4 copy.54
  365.2 1.7 copy-done
  366.9 0.4 copy.55
  367.3 6.2 %fusion.7 = f32[2048,128,4,1]{1,2,3,0:T(4,128)S(1)} fusion(bf16[4,2,2,2048]{0,1,2,3:T(2,128)(2,1)S(1)} %copy-done.2, bf16[128,2,1,2048]{0,1,2,3:T(2,128)(2,1)S(1)} %get-tuple-element.45, bf16[128,2,1,2048]{0,1,2,3:T(2,128)(2,1)S(1)} %get-tuple-element.44), kind=kOutput, calls=%fused_computation.14 | convolution fusion | flops 12582912 | bytes 6356992 | tf_op jit(solution)/shard_map/while/body/eval_jaxpr/iscf,jscf->ijf/dot_general | solution.py:50
  373.6 0.4 copy.52
  374.0 0.0 copy-start.3
  374.0 0.4 copy.53
  374.5 0.8 copy-done.3
  375.2 1.3 fusion.9
  376.6 1.3 fusion.12
  377.9 0.7 pad_maximum_fusion.4
  (10 shorter events, 0.1 us)
Async XLA Ops:
  6.5 30.4 %copy-start.6 = (s32[2,512]{1,0:T(2,128)S(1)}, s32[2,512]{1,0:T(2,128)}, u32[]{:S(2)}) copy-start(s32[2,512]{1,0:T(2,128)} %param.3) | copy-start | bytes 12292
  6.5 176.6 %all-gather.3.cloned.1.call-start = ((), (), s32[]{:S(2)}) async-start(), calls=%async_computation | async-start | bytes 2162688 | tf_op jit(solution)/shard_map/all_gather | solution.py:99
  9.6 5.6 %collective-permute-start = (bf16[4,2,2,2048]{3,0,2,1:T(4,128)(2,1)S(1)}, bf16[4,2,2,2048]{3,0,2,1:T(4,128)(2,1)S(1)}, u32[]{:S(2)}, u32[]{:S(2)}) collective-permute-start(bf16[4,2,2,2048]{3,0,2,1:T(4,128)(2,1)S(1)} %fusion.26), channel_id=1, source_target_pairs={{480,0},{0,32},{32,64},{64,96},{96,128},{128,160},{160,192},{192,2... | collective-permute-start | bytes 196616 | tf_op jit(solution)/shard_map/ppermute | solution.py:15
  15.9 326.9 %all-gather.5.cloned.1.call-start = ((), (), s32[]{:S(2)}) async-start(), calls=%async_computation.1 | async-start | bytes 2162688 | tf_op jit(solution)/shard_map/all_gather | solution.py:99
  16.0 16.0 %collective-permute-start.1 = (bf16[4,2,2,2048]{3,0,2,1:T(4,128)(2,1)S(1)}, bf16[4,2,2,2048]{3,0,2,1:T(4,128)(2,1)S(1)}, u32[]{:S(2)}, u32[]{:S(2)}) collective-permute-start(bf16[4,2,2,2048]{3,0,2,1:T(4,128)(2,1)S(1)} %fusion.26), channel_id=1, source_target_pairs={{448,0},{480,32},{0,64},{32,96},{64,128},{96,160},{128,192},{160,2... | collective-permute-start | bytes 196616 | tf_op jit(solution)/shard_map/ppermute | solution.py:15
  192.0 2.6 copy-start.1
  351.7 1.7 copy-start.2
  353.3 5.3 %copy-start.4 = (bf16[128,2,1,2048]{0,1,2,3:T(2,128)(2,1)S(1)}, bf16[128,2,1,2048]{0,1,2,3:T(2,128)(2,1)}, u32[]{:S(2)}) copy-start(bf16[128,2,1,2048]{0,1,2,3:T(2,128)(2,1)} %get-tuple-element.42) | copy-start | bytes 3145732
  353.3 5.3 %copy-start.5 = (bf16[128,2,1,2048]{0,1,2,3:T(2,128)(2,1)S(1)}, bf16[128,2,1,2048]{0,1,2,3:T(2,128)(2,1)}, u32[]{:S(2)}) copy-start(bf16[128,2,1,2048]{0,1,2,3:T(2,128)(2,1)} %get-tuple-element.43) | copy-start | bytes 3145732
  364.7 2.2 copy-start
  374.0 1.2 copy-start.3
Sparse Core Ops, SparseCore 0:
  16.1 167.0 all-gather.2
  185.3 157.4 all-gather.4
where the time goes:
time: 386 us
  waiting for transfers between devices  287 us (74%)
  local copies, waits for them, and re-layouts  27.4 us (7%)
  matrix products  27.2 us (7%)
  starting transfers between devices  16.1 us (4%)
  other arithmetic  13.7 us (4%)
  between operations  13.7 us (4%)
    all_gather x2, waiting for transfers between devices, local(): lax.all_gather(partner, 'dev', axis=0, tiled=True)  282 us
    all_gather x2, local copies, waits for them, and re-layouts, local(): lax.all_gather(partner, 'dev', axis=0, tiled=True)  17.7 us
    ppermute x2, starting transfers between devices, from_behind(): return lax.ppermute(block, axis, route)  16.1 us
    dot_general x2, matrix products, pair_slab(): jnp.einsum('iscf,jscf->ijf', left_block, swapped, preferred_element_type=...  12.2 us
    dot_general x2, matrix products, pair_slab(): jnp.einsum('iscf,jscf->ijf', left_block, right_block, preferred_element_t...  11.9 us
  transfers between devices with their start and end apart: 4, of which 4 were waited for; matrix products, arithmetic and copies ran while one was open for 7% of the time, Pallas kernels for 0%

commit v1 on v0

v1 whole, which is shorter than its diff:
```python
import functools
import math

import jax
import jax.numpy as jnp
import ml_dtypes
import numpy as np
from jax import lax
from jax.experimental import pallas as pl
from jax.experimental.pallas import tpu as pltpu
from jax.sharding import PartitionSpec as P

LAGS = 128
ROUNDS = 2
NZ = 8
NY = 4
NG = 16
CH = 4
BINS = 2048
TILE = 128
MESH = pl.DeviceIdType.MESH


def lag_table():
    frequency = np.arange(BINS, dtype=np.int64)
    lag_index = np.arange(LAGS, dtype=np.int64) - LAGS // 2
    turns = np.mod(frequency[:, None] * lag_index[None, :], 2 * BINS)
    angles = turns * (math.pi / BINS)
    table = np.concatenate([np.cos(angles), -np.sin(angles)], 0) / math.sqrt(BINS)
    return table.astype(np.float32).astype(ml_dtypes.bfloat16)


def kernel(
    spectra_ref, counts_ref, table_ref, out_ref,
    raw, white, left, left_f32, right, partner, table, products, pieces,
    local_sem, left_send, left_recv, right_send, right_recv, pass_send, out_send, out_recv,
):
    g = lax.axis_index("grp")
    d = lax.axis_index("dev")
    z = d // NY
    y = d % NY
    core = g % 2

    load_raw = pltpu.make_async_copy(spectra_ref, raw, local_sem.at[0])
    load_raw.start()
    load_table = pltpu.make_async_copy(table_ref, table, local_sem.at[1])
    load_table.start()

    def ring(step):
        return (g, ((z + step + NZ) % NZ) * NY + y)

    def line(group_step, line_y):
        return ((g + group_step + NG) % NG, z * NY + line_y)

    barrier = pltpu.get_barrier_semaphore()

    def greet(device):
        pl.semaphore_signal(barrier, inc=1, device_id=device, device_id_type=MESH)

    for step in range(1, NZ):
        greet(ring(step))
    for other in range(NY):
        greet(line(-1, other))

    @pl.when(core == 0)
    def _():
        for other in range(NY):
            greet(line(-2, other))

    load_raw.wait()
    block = g * (NZ * NY) + d
    for ch in range(CH):
        for s in range(2):
            x = raw[ch, s]
            energy = jnp.sum(x * x) * (1.0 / (2 * BINS))
            live = jnp.where(counts_ref[s, block] > ch, 1.0, 0.0).astype(jnp.float32)
            scale = live / jnp.sqrt(jnp.full((1, BINS), energy + 1e-06, jnp.float32))
            left_f32[s * 8 + ch : s * 8 + ch + 1, :] = x[0:1] * scale
            left_f32[s * 8 + 4 + ch : s * 8 + 4 + ch + 1, :] = x[1:2] * scale
    white[...] = left_f32[...].astype(jnp.bfloat16)

    @pl.when(core == 0)
    def _():
        pl.semaphore_wait(barrier, NZ - 1 + 2 * NY)

    @pl.when(core == 1)
    def _():
        pl.semaphore_wait(barrier, NZ - 1 + NY)

    def left_copy(source, slot, step):
        return pltpu.make_async_remote_copy(
            src_ref=source, dst_ref=left.at[slot],
            send_sem=left_send.at[slot], recv_sem=left_recv.at[slot],
            device_id=ring(step), device_id_type=MESH,
        )

    def half_copy(source_slot, half, step):
        columns = pl.ds(half * (BINS // 2), BINS // 2)
        return pltpu.make_async_remote_copy(
            src_ref=left.at[source_slot, :, columns], dst_ref=left.at[NZ - 1, :, columns],
            send_sem=left_send.at[NZ - 1 + half], recv_sem=left_recv.at[NZ - 1 + half],
            device_id=ring(step), device_id_type=MESH,
        )

    def right_copy(k, other):
        return pltpu.make_async_remote_copy(
            src_ref=white, dst_ref=right.at[k, y],
            send_sem=right_send.at[k, other], recv_sem=right_recv.at[k, y],
            device_id=line(k + 1, other), device_id_type=MESH,
        )

    def right_arrival(k, other):
        return pltpu.make_async_remote_copy(
            src_ref=white, dst_ref=right.at[k, other],
            send_sem=right_send.at[k, other], recv_sem=right_recv.at[k, other],
            device_id=line(k + 1, other), device_id_type=MESH,
        )

    def pass_copy(other):
        return pltpu.make_async_remote_copy(
            src_ref=right.at[0, other], dst_ref=right.at[1, other],
            send_sem=pass_send.at[other], recv_sem=right_recv.at[1, other],
            device_id=line(1, y), device_id_type=MESH,
        )

    left_copy(white, 1, 1).start()
    left_copy(white, 2, -1).start()
    for other in range(NY):
        right_copy(0, other).start()

    @pl.when(core == 0)
    def _():
        for other in range(NY):
            right_copy(1, other).start()

    for n in range(1, NZ // 2):
        for slot, step in ((2 * n - 1, 1), (2 * n, -1)):
            left_copy(white, slot, step).wait_recv()
            if n < NZ // 2 - 1:
                left_copy(left.at[slot], slot + 2, step).start()
            else:
                half_copy(slot, (1 - step) // 2, step).start()
    for other in range(NY):
        right_arrival(0, other).wait_recv()

        @pl.when(core == 0)
        def _():
            pass_copy(other).start()

    def gather(k):
        def body(t, carry):
            columns = pl.ds(pl.multiple_of(t * TILE, TILE), TILE)
            parts = [right[k, other, :, columns].astype(jnp.float32) for other in range(NY)]
            for sc in range(4):
                rows = jnp.concatenate([p[4 * sc : 4 * sc + 4] for p in parts], axis=0)
                partner[k, sc, :, columns] = rows.astype(jnp.bfloat16)
            return carry

        lax.fori_loop(0, BINS // TILE, body, 0)

    gather(0)
    for other in range(NY):
        right_arrival(1, other).wait_recv()
    gather(1)
    load_table.wait()

    row = lax.broadcasted_iota(jnp.int32, (NY * CH, LAGS), 0)
    both = []
    for k in range(ROUNDS):
        partner_first = ((g - 1 - k + NG) % NG) * (NZ * NY) + z * NY
        limit = jnp.zeros((NY * CH, LAGS), jnp.int32)
        for other in range(NY):
            least = jnp.minimum(
                counts_ref[0, partner_first + other], counts_ref[1, partner_first + other]
            )
            limit = jnp.where(row // CH == other, least, limit)
        both.append(jnp.where(row % CH < limit, 0.5, 0.0).astype(jnp.float32))

    def out_copy(slot, other_slot, owner_z, land_z):
        return pltpu.make_async_remote_copy(
            src_ref=pieces.at[slot],
            dst_ref=out_ref.at[:, :, pl.ds(pl.multiple_of(land_z * 16, 16), 16), :],
            send_sem=out_send.at[slot], recv_sem=out_recv.at[other_slot],
            device_id=(g, owner_z * NY + y), device_id_type=MESH,
        )

    def mate(slot):
        return jnp.where(slot == NZ - 1, slot, jnp.where(slot % 2 == 1, slot + 1, slot - 1))

    def source_z(slot):
        step = jnp.where(slot % 2 == 1, NZ - (slot + 1) // 2, slot // 2)
        return (z + step) % NZ

    def one_block(slot, carry):
        @pl.when(slot == NZ - 1)
        def _():
            half_copy(1, 0, 1).wait_recv()
            half_copy(2, 1, -1).wait_recv()

        @pl.when(slot == 0)
        def _():
            left_f32[...] = white[...].astype(jnp.float32)

        @pl.when(slot > 0)
        def _():
            left_f32[...] = left[slot].astype(jnp.float32)

        def tile(t, inner):
            at = pl.multiple_of(t * TILE, TILE)
            columns = pl.ds(at, TILE)
            imag_columns = pl.ds(pl.multiple_of(BINS + at, TILE), TILE)
            theirs = [[partner[k, sc, :, columns] for sc in range(4)] for k in range(ROUNDS)]
            for ch in range(CH):
                mine = [
                    jnp.broadcast_to(
                        left_f32[4 * sc + ch : 4 * sc + ch + 1, columns], (16, TILE)
                    ).astype(jnp.bfloat16)
                    for sc in range(4)
                ]
                for k in range(ROUNDS):
                    a0, b0, a1, b1 = theirs[k]
                    ma0, mb0, ma1, mb1 = mine
                    real = (ma0 * a0 + mb0 * b0) + (ma1 * a1 + mb1 * b1)
                    imag = (mb0 * a0 - ma0 * b0) + (mb1 * a1 - ma1 * b1)
                    at_row = (k * CH + ch) * 16
                    products[at_row : at_row + 16, columns] = real
                    products[at_row : at_row + 16, imag_columns] = imag
            return inner

        lax.fori_loop(0, BINS // TILE, tile, 0)
        lagged = jnp.dot(products[...], table[...], preferred_element_type=jnp.float32)
        owner = source_z(slot)
        mine_block = g * (NZ * NY) + owner * NY + y
        least = jnp.minimum(counts_ref[0, mine_block], counts_ref[1, mine_block])
        for ch in range(CH):
            factor = jnp.where(least > ch, 1.0, 0.0).astype(jnp.float32)
            for k in range(ROUNDS):
                at_row = (k * CH + ch) * 16
                scale = 1.0 - both[k] * factor
                pieces[slot, k, ch] = (lagged[at_row : at_row + 16] * scale).astype(jnp.bfloat16)

        @pl.when(slot == 0)
        def _():
            pltpu.make_async_copy(
                pieces.at[0],
                out_ref.at[:, :, pl.ds(pl.multiple_of(z * 16, 16), 16), :],
                local_sem.at[2],
            ).start()

        @pl.when(slot > 0)
        def _():
            out_copy(slot, mate(slot), owner, z).start()

        return carry

    lax.fori_loop(0, NZ, one_block, 0)

    def finish(slot, carry):
        out_copy(slot, slot, source_z(slot), source_z(slot)).wait_recv()
        out_copy(slot, slot, source_z(slot), source_z(slot)).wait_send()
        return carry

    lax.fori_loop(1, NZ, finish, 0)
    pltpu.make_async_copy(
        pieces.at[0],
        out_ref.at[:, :, pl.ds(pl.multiple_of(z * 16, 16), 16), :],
        local_sem.at[2],
    ).wait()
    for slot in range(1, NZ - 1):
        left_copy(white, slot, 1).wait_send()
    half_copy(1, 0, 1).wait_send()
    half_copy(2, 1, -1).wait_send()
    for other in range(NY):
        right_copy(0, other).wait_send()

    @pl.when(core == 0)
    def _():
        for other in range(NY):
            right_copy(1, other).wait_send()
            pass_copy(other).wait_send()


def local(spectra, counts, table):
    bf16 = jnp.bfloat16
    dma = pltpu.SemaphoreType.DMA
    return pl.pallas_call(
        kernel,
        out_shape=jax.ShapeDtypeStruct((ROUNDS, CH, NZ * NY * CH, LAGS), bf16),
        in_specs=[
            pl.BlockSpec(memory_space=pl.ANY),
            pl.BlockSpec(memory_space=pltpu.SMEM),
            pl.BlockSpec(memory_space=pl.ANY),
        ],
        out_specs=pl.BlockSpec(memory_space=pl.ANY),
        scratch_shapes=[
            pltpu.VMEM((CH, 2, 2, BINS), jnp.float32),
            pltpu.VMEM((16, BINS), bf16),
            pltpu.VMEM((NZ, 16, BINS), bf16),
            pltpu.VMEM((16, BINS), jnp.float32),
            pltpu.VMEM((ROUNDS, NY, 16, BINS), bf16),
            pltpu.VMEM((ROUNDS, 4, 16, BINS), bf16),
            pltpu.VMEM((2 * BINS, LAGS), bf16),
            pltpu.VMEM((ROUNDS * CH * 16, 2 * BINS), bf16),
            pltpu.VMEM((NZ, ROUNDS, CH, 16, LAGS), bf16),
            dma((3,)),
            dma((NZ + 1,)),
            dma((NZ + 1,)),
            dma((ROUNDS, NY)),
            dma((ROUNDS, NY)),
            dma((NY,)),
            dma((NZ,)),
            dma((NZ,)),
        ],
        compiler_params=pltpu.CompilerParams(
            collective_id=0, has_side_effects=True, vmem_limit_bytes=32 * 1024 * 1024
        ),
        cost_estimate=pl.CostEstimate(
            flops=1100000000, bytes_accessed=1600000, transcendentals=0
        ),
    )(spectra, counts, table)


def solution(mesh):
    table = lag_table()

    def whole(spectra, counts):
        return jax.shard_map(
            local,
            mesh=mesh,
            in_specs=(P(("grp", "dev"), None, None, None), P(), P()),
            out_specs=P(None, ("grp", "dev"), None, None),
            check_vma=False,
        )(spectra, counts, jnp.asarray(table))

    return whole
```

time: 386 us -> 47.1 us (0.12)
  the two profiles are of different devices: /device:TPU:6 before, /device:TPU:17 now
where the time goes in v1:
time: 47.1 us; the launch traced here: 46.9 us
  Pallas kernels  43.4 us (92%)
  local copies, waits for them, and re-layouts  3.52 us (7%)
    pallas_call x1, Pallas kernels, local(): pl.pallas_call(kernel, out_shape=jax.ShapeDtypeStruct((ROUNDS, CH, NZ * N...  43.4 us
    unnamed x7, local copies, waits for them, and re-layouts  3.52 us

profile of v1, /device:TPU:17, one launch (start us, length us, event | category | flops | bytes accessed | tf_op | source)
XLA Modules:
  0.0 46.9 jit_solution(12867256127730776893)
XLA Ops:
  0.0 0.0 copy-start
  0.0 0.9 %copy-done = f32[4,2,2,2048]{3,2,1,0:T(2,128)S(1)} copy-done((f32[4,2,2,2048]{3,2,1,0:T(2,128)S(1)}, f32[4,2,2,2048]{3,2,1,0:T(2,128)}, u32[]{:S(2)}) %copy-start) | copy-done | bytes 131096
  0.9 0.0 copy-start.1
  0.9 0.7 %copy-done.1 = s32[2,512]{1,0:T(2,128)S(1)} copy-done((s32[2,512]{1,0:T(2,128)S(1)}, s32[2,512]{1,0:T(2,128)}, u32[]{:S(2)}) %copy-start.1) | copy-done | bytes 4120
  1.6 0.0 copy-start.2
  1.6 1.2 %copy-done.2 = bf16[4096,128]{1,0:T(8,128)(2,1)S(1)} copy-done((bf16[4096,128]{1,0:T(8,128)(2,1)S(1)}, bf16[4096,128]{1,0:T(8,128)(2,1)}, u32[]{:S(2)}) %copy-start.2) | copy-done | bytes 1048600
  2.8 43.4 %shard_map.37 = bf16[2,4,128,128]{3,2,1,0:T(8,128)(2,1)S(1)} custom-call(f32[4,2,2,2048]{3,2,1,0:T(2,128)S(1)} %copy-done, s32[2,512]{1,0:T(2,128)S(1)} %copy-done.1, bf16[4096,128]{1,0:T(8,128)(2,1)S(1)} %copy-done.2), custom_call_target="tpu_custom_call" | custom-call | flops 1100000000 | bytes 1600000 | tf_op jit(solution)/shard_map/pallas_call | solution.py:286
  46.2 0.7 %copy.5 = bf16[2,4,128,128]{3,2,1,0:T(8,128)(2,1)} copy(bf16[2,4,128,128]{3,2,1,0:T(8,128)(2,1)S(1)} %shard_map.37) | data formatting | bytes 524288
Async XLA Ops:
  0.0 0.9 %copy-start = (f32[4,2,2,2048]{3,2,1,0:T(2,128)S(1)}, f32[4,2,2,2048]{3,2,1,0:T(2,128)}, u32[]{:S(2)}) copy-start(f32[4,2,2,2048]{3,2,1,0:T(2,128)} %spectra_ref.1) | copy-start | bytes 393220
  0.9 0.7 %copy-start.1 = (s32[2,512]{1,0:T(2,128)S(1)}, s32[2,512]{1,0:T(2,128)}, u32[]{:S(2)}) copy-start(s32[2,512]{1,0:T(2,128)} %counts_ref.1) | copy-start | bytes 12292
  1.6 1.2 %copy-start.2 = (bf16[4096,128]{1,0:T(8,128)(2,1)S(1)}, bf16[4096,128]{1,0:T(8,128)(2,1)}, u32[]{:S(2)}) copy-start(bf16[4096,128]{1,0:T(8,128)(2,1)} %constant.2.clone.table_ref) | copy-start | bytes 3145732

commit v2 on v0

v2 whole, which is shorter than its diff:
```python
import math

import jax
import jax.numpy as jnp
import ml_dtypes
import numpy as np
from jax import lax
from jax.experimental import pallas as pl
from jax.experimental.pallas import tpu as pltpu
from jax.sharding import PartitionSpec as P

LAGS = 128
ROUNDS = 2
NZ = 8
NY = 4
NG = 16
NX = 4
CH = 4
BINS = 2048
TILE = 128
TILES = BINS // TILE
PEERS = 2 * NY
MESH = pl.DeviceIdType.MESH


def lag_table():
    frequency = np.arange(BINS, dtype=np.int64)
    lag_index = np.arange(LAGS, dtype=np.int64) - LAGS // 2
    turns = np.mod(frequency[:, None] * lag_index[None, :], 2 * BINS)
    angles = turns * (math.pi / BINS)
    table = np.stack([np.cos(angles), -np.sin(angles)], 0) / math.sqrt(BINS)
    table = table.reshape(2, TILES, TILE, LAGS).transpose(1, 0, 2, 3).reshape(2 * BINS, LAGS)
    return table.astype(np.float32).astype(ml_dtypes.bfloat16)


def kernel(
    spectra_ref, counts_hbm, table_ref, out_ref,
    raw, counts, white, wide_f32, left, left_wide, right, partner, table, pieces, landed, result,
    local_sem, late_sem, left_send, left_recv, right_recv, import_send, along_send, mate_send,
    out_send, out_recv,
):
    g = lax.axis_index("grp")
    d = lax.axis_index("dev")
    z = d // NY
    y = d % NY
    core = g % 2
    x = (g // 2) % NX
    parity = z % 2
    q = z // 2
    late = q >= 2
    me = parity * NY + y
    mate_g = g + 1 - 2 * core

    load_raw = pltpu.make_async_copy(spectra_ref, raw, local_sem.at[0])
    load_raw.start()
    load_counts = pltpu.make_async_copy(counts_hbm, counts, local_sem.at[1])
    load_counts.start()
    load_table = pltpu.make_async_copy(table_ref, table, local_sem.at[2])
    load_table.start()

    def peer(slot):
        return (g, (2 * q + slot // NY) * NY + slot % NY)

    def row(other_q, group):
        return (group, (parity + 2 * other_q) * NY + y)

    beside = q + 1 - 2 * (q % 2)
    far = [(q + 2) % 4, (beside + 2) % 4]
    mate = (mate_g, d)
    mirrored = z * NY + (NY - 1 - y)
    import_to = ((g + 2) % NG, jnp.where(x == NX - 1, mirrored, d))
    import_from = ((g - 2 + NG) % NG, jnp.where(x == 0, mirrored, d))

    barrier = pltpu.get_barrier_semaphore()

    def greet(device, semaphore=barrier):
        pl.semaphore_signal(semaphore, inc=1, device_id=device, device_id_type=MESH)

    @pl.when(jnp.logical_not(late))
    def _():
        for other in far:
            greet(row(other, g))
            greet(row(other, mate_g))

    greet(import_from)
    for step in range(1, PEERS):
        greet(peer((me + step) % PEERS))
    greet(mate)
    greet(row(beside, g))
    greet(row(beside, mate_g))

    near = 1 + (PEERS - 1) + 1 + 2

    load_counts.wait()
    load_raw.wait()
    block = g * (NZ * NY) + d
    for ch in range(CH):
        for s in range(2):
            values = raw[ch, s]
            energy = jnp.sum(values * values) * (1.0 / (2 * BINS))
            live = jnp.where(counts[s, block] > ch, 1.0, 0.0).astype(jnp.float32)
            scale = live / jnp.sqrt(jnp.full((1, BINS), energy + 1e-06, jnp.float32))
            wide_f32[s * 8 + ch : s * 8 + ch + 1, :] = values[0:1] * scale
            wide_f32[s * 8 + 4 + ch : s * 8 + 4 + ch + 1, :] = values[1:2] * scale
    white[...] = wide_f32[...].astype(jnp.bfloat16)

    @pl.when(jnp.logical_not(late))
    def _():
        pl.semaphore_wait(barrier, near)

    @pl.when(late)
    def _():
        pl.semaphore_wait(barrier, near + 4)
        for other in far:
            greet(row(other, g), late_sem)
            greet(row(other, mate_g), late_sem)

    def import_copy():
        return pltpu.make_async_remote_copy(
            src_ref=white, dst_ref=right.at[1, q],
            send_sem=import_send, recv_sem=right_recv.at[1, q],
            device_id=import_to, device_id_type=MESH,
        )

    def along_copy(n, other):
        return pltpu.make_async_remote_copy(
            src_ref=right.at[1, q], dst_ref=right.at[1, q],
            send_sem=along_send.at[n], recv_sem=right_recv.at[1, q],
            device_id=row(other, g), device_id_type=MESH,
        )

    def own_copy(n, other):
        return pltpu.make_async_remote_copy(
            src_ref=white, dst_ref=right.at[0, q],
            send_sem=mate_send.at[n], recv_sem=right_recv.at[0, q],
            device_id=row(other, mate_g), device_id_type=MESH,
        )

    def mate_copy(n, other):
        return pltpu.make_async_remote_copy(
            src_ref=right.at[1, other], dst_ref=right.at[0, other],
            send_sem=mate_send.at[n], recv_sem=right_recv.at[0, other],
            device_id=mate, device_id_type=MESH,
        )

    def arrival(k, other):
        return pltpu.make_async_remote_copy(
            src_ref=white, dst_ref=right.at[k, other],
            send_sem=import_send, recv_sem=right_recv.at[k, other],
            device_id=mate, device_id_type=MESH,
        )

    def left_copy(n, slot):
        return pltpu.make_async_remote_copy(
            src_ref=white, dst_ref=left.at[me],
            send_sem=left_send.at[n], recv_sem=left_recv.at[me],
            device_id=peer(slot), device_id_type=MESH,
        )

    def left_arrival(slot):
        return pltpu.make_async_remote_copy(
            src_ref=white, dst_ref=left.at[slot],
            send_sem=left_send.at[0], recv_sem=left_recv.at[slot],
            device_id=peer(slot), device_id_type=MESH,
        )

    import_copy().start()

    @pl.when(jnp.logical_and(core == 0, late))
    def _():
        own_copy(2, far[0]).start()
        own_copy(3, far[1]).start()

    @pl.when(core == 0)
    def _():
        own_copy(0, q).start()
        own_copy(1, beside).start()

    for n in range(PEERS - 1):
        left_copy(n, (me + 1 + n) % PEERS).start()

    arrival(1, q).wait_recv()

    @pl.when(late)
    def _():
        along_copy(1, far[0]).start()
        along_copy(2, far[1]).start()

    along_copy(0, beside).start()

    @pl.when(core == 1)
    def _():
        mate_copy(0, q).start()

    @pl.when(jnp.logical_not(late))
    def _():
        pl.semaphore_wait(late_sem, 4)

        @pl.when(core == 0)
        def _():
            own_copy(2, far[0]).start()
            own_copy(3, far[1]).start()

        along_copy(1, far[0]).start()
        along_copy(2, far[1]).start()

    def widen(n, carry):
        slot = (me + n) % PEERS

        @pl.when(n > 0)
        def _():
            left_arrival(slot).wait_recv()
            wide_f32[...] = left[slot].astype(jnp.float32)

        def tile(t, inner):
            columns = pl.ds(pl.multiple_of(t * TILE, TILE), TILE)
            for r in range(16):
                left_wide[slot * 16 + r, :, columns] = jnp.broadcast_to(
                    wide_f32[r : r + 1, columns], (16, TILE)
                ).astype(jnp.bfloat16)
            return inner

        lax.fori_loop(0, TILES, tile, 0)
        return carry

    lax.fori_loop(0, PEERS, widen, 0)
    load_table.wait()

    mirror = x == 0
    flip = [jnp.logical_and(mirror, core == 0), mirror]
    row_id = lax.broadcasted_iota(jnp.int32, (16, LAGS), 0)

    def out_copy(e, n, slot):
        return pltpu.make_async_remote_copy(
            src_ref=pieces.at[e, slot], dst_ref=landed.at[e, me],
            send_sem=out_send.at[e, n], recv_sem=out_recv.at[e, me],
            device_id=peer(slot), device_id_type=MESH,
        )

    def out_arrival(e, slot):
        return pltpu.make_async_remote_copy(
            src_ref=pieces.at[e, slot], dst_ref=landed.at[e, slot],
            send_sem=out_send.at[e, 0], recv_sem=out_recv.at[e, slot],
            device_id=peer(slot), device_id_type=MESH,
        )

    def half(e, carry):
        for zz in range(2):
            other = 2 * e + zz

            @pl.when(other != q)
            def _():
                arrival(1, other).wait_recv()

                @pl.when(core == 1)
                def _():
                    mate_copy((other - q + 4) % 4, other).start()

        for zz in range(2):
            arrival(0, 2 * e + zz).wait_recv()

        def gather(t, inner):
            columns = pl.ds(pl.multiple_of(t * TILE, TILE), TILE)
            parts = [
                right[k, 2 * e + zz, :, columns].astype(jnp.float32)
                for k in range(ROUNDS)
                for zz in range(2)
            ]
            for sc in range(4):
                rows = jnp.concatenate([p[4 * sc : 4 * sc + 4] for p in parts], axis=0)
                partner[sc, :, columns] = rows.astype(jnp.bfloat16)
            return inner

        lax.fori_loop(0, TILES, gather, 0)

        limit = jnp.zeros((16, LAGS), jnp.int32)
        for k in range(ROUNDS):
            column = jnp.where(flip[k], NY - 1 - y, y)
            for zz in range(2):
                group = (g - 1 - k + NG) % NG
                at = group * (NZ * NY) + (parity + 2 * (2 * e + zz)) * NY + column
                least = jnp.minimum(counts[0, at], counts[1, at])
                limit = jnp.where(row_id // 4 == k * 2 + zz, least, limit)
        both = jnp.where(row_id % 4 < limit, 0.5, 0.0).astype(jnp.float32)

        def owners(n, inner):
            slots = [(me + 1 + 2 * n + i) % PEERS for i in range(2)]

            def tile(t, acc):
                columns = pl.ds(pl.multiple_of(t * TILE, TILE), TILE)
                a0, b0, a1, b1 = [partner[sc, :, columns] for sc in range(4)]
                products = []
                for slot in slots:
                    for ch in range(CH):
                        ma0, mb0, ma1, mb1 = [
                            left_wide[slot * 16 + 4 * sc + ch, :, columns] for sc in range(4)
                        ]
                        real = (ma0 * a0 + mb0 * b0) + (ma1 * a1 + mb1 * b1)
                        imag = (mb0 * a0 - ma0 * b0) + (mb1 * a1 - ma1 * b1)
                        products.append(jnp.concatenate([real, imag], axis=1))
                rows = pl.ds(pl.multiple_of(t * 2 * TILE, 2 * TILE), 2 * TILE)
                return acc + jnp.dot(
                    jnp.concatenate(products, axis=0),
                    table[rows, :],
                    preferred_element_type=jnp.float32,
                )

            lagged = lax.fori_loop(
                0, TILES, tile, jnp.zeros((2 * CH * 16, LAGS), jnp.float32), unroll=2
            )
            for i, slot in enumerate(slots):
                at = g * (NZ * NY) + (2 * q + slot // NY) * NY + slot % NY
                least = jnp.minimum(counts[0, at], counts[1, at])
                for ch in range(CH):
                    factor = jnp.where(least > ch, 1.0, 0.0).astype(jnp.float32)
                    first = (i * CH + ch) * 16
                    pieces[e, slot, ch] = (
                        lagged[first : first + 16] * (1.0 - both * factor)
                    ).astype(jnp.bfloat16)
            out_copy(e, 2 * n, slots[0]).start()

            @pl.when(n < PEERS // 2 - 1)
            def _():
                out_copy(e, 2 * n + 1, slots[1]).start()

            return inner

        lax.fori_loop(0, PEERS // 2, owners, 0)
        return carry

    lax.fori_loop(0, 2, half, 0)

    def store(e):
        return pltpu.make_async_copy(
            result.at[:, :, pl.ds(e * 64, 64), :],
            out_ref.at[:, :, pl.ds(e * 64, 64), :],
            local_sem.at[3 + e],
        )

    for e in range(2):
        for n in range(PEERS - 1):
            out_arrival(e, (me + 1 + n) % PEERS).wait_recv()
        landed[e, me] = pieces[e, me]

        def assemble(n, carry, e=e):
            side = n // CH
            ch = n % CH
            for k in range(ROUNDS):
                parts = []
                for column in range(NY):
                    source = jnp.where(flip[k], NY - 1 - column, column)
                    tile = landed[e, side * NY + source, ch].astype(jnp.float32)
                    parts.append(tile[8 * k : 8 * k + 8])
                for zz in range(2):
                    rows = jnp.concatenate([p[4 * zz : 4 * zz + 4] for p in parts], axis=0)
                    at = pl.multiple_of((side + 4 * e + 2 * zz) * 16, 16)
                    result[k, ch, pl.ds(at, 16), :] = rows.astype(jnp.bfloat16)
            return carry

        lax.fori_loop(0, 2 * CH, assemble, 0)
        store(e).start()

    import_copy().wait_send()
    for n in range(PEERS - 1):
        left_copy(n, (me + 1 + n) % PEERS).wait_send()
        for e in range(2):
            out_copy(e, n, (me + 1 + n) % PEERS).wait_send()
    along_copy(0, beside).wait_send()
    along_copy(1, far[0]).wait_send()
    along_copy(2, far[1]).wait_send()

    @pl.when(core == 0)
    def _():
        own_copy(0, q).wait_send()
        own_copy(1, beside).wait_send()
        own_copy(2, far[0]).wait_send()
        own_copy(3, far[1]).wait_send()

    @pl.when(core == 1)
    def _():
        for n in range(4):
            mate_copy(n, (q + n) % 4).wait_send()

    store(0).wait()
    store(1).wait()


def local(spectra, counts, table):
    bf16 = jnp.bfloat16
    dma = pltpu.SemaphoreType.DMA
    return pl.pallas_call(
        kernel,
        out_shape=jax.ShapeDtypeStruct((ROUNDS, CH, NZ * NY * CH, LAGS), bf16),
        in_specs=[pl.BlockSpec(memory_space=pl.ANY)] * 3,
        out_specs=pl.BlockSpec(memory_space=pl.ANY),
        scratch_shapes=[
            pltpu.VMEM((CH, 2, 2, BINS), jnp.float32),
            pltpu.SMEM(counts.shape, jnp.int32),
            pltpu.VMEM((16, BINS), bf16),
            pltpu.VMEM((16, BINS), jnp.float32),
            pltpu.VMEM((PEERS, 16, BINS), bf16),
            pltpu.VMEM((PEERS * 16, 16, BINS), bf16),
            pltpu.VMEM((ROUNDS, 4, 16, BINS), bf16),
            pltpu.VMEM((4, 16, BINS), bf16),
            pltpu.VMEM((2 * BINS, LAGS), bf16),
            pltpu.VMEM((2, PEERS, CH, 16, LAGS), bf16),
            pltpu.VMEM((2, PEERS, CH, 16, LAGS), bf16),
            pltpu.VMEM((ROUNDS, CH, NZ * NY * CH, LAGS), bf16),
            dma((5,)),
            pltpu.SemaphoreType.REGULAR,
            dma((PEERS - 1,)),
            dma((PEERS,)),
            dma((ROUNDS, 4)),
            dma,
            dma((3,)),
            dma((4,)),
            dma((2, PEERS - 1)),
            dma((2, PEERS)),
        ],
        compiler_params=pltpu.CompilerParams(
            collective_id=0, has_side_effects=True, vmem_limit_bytes=60 * 1024 * 1024
        ),
        cost_estimate=pl.CostEstimate(
            flops=1100000000, bytes_accessed=1600000, transcendentals=0
        ),
    )(spectra, counts, table)


def solution(mesh):
    table = lag_table()

    def whole(spectra, counts):
        return jax.shard_map(
            local,
            mesh=mesh,
            in_specs=(P(("grp", "dev"), None, None, None), P(), P()),
            out_specs=P(None, ("grp", "dev"), None, None),
            check_vma=False,
        )(spectra, counts, jnp.asarray(table))

    return whole
```

time: 386 us -> 45.6 us (0.12)
  the two profiles are of different devices: /device:TPU:6 before, /device:TPU:8 now
where the time goes in v2:
time: 45.6 us; the launch traced here: 45.4 us
  Pallas kernels  43.7 us (96%)
  local copies, waits for them, and re-layouts  1.67 us (4%)
    pallas_call x1, Pallas kernels, local(): pl.pallas_call(kernel, out_shape=jax.ShapeDtypeStruct((ROUNDS, CH, NZ * N...  43.7 us
    unnamed x1, local copies, waits for them, and re-layouts  1.67 us

profile of v2, /device:TPU:8, one launch (start us, length us, event | category | flops | bytes accessed | tf_op | source)
XLA Modules:
  0.0 45.4 jit_solution(5310259180856708904)
XLA Ops:
  0.0 43.7 %shard_map.37 = bf16[2,4,128,128]{3,2,1,0:T(8,128)(2,1)} custom-call(f32[4,2,2,2048]{3,2,1,0:T(2,128)} %spectra_ref.1, s32[2,512]{1,0:T(2,128)} %counts_hbm.1, bf16[4096,128]{1,0:T(8,128)(2,1)} %constant.2.clone.table_ref), custom_call_target="tpu_custom_call" | custom-call | flops 1100000000 | bytes 1600000 | tf_op jit(solution)/shard_map/pallas_call | solution.py:391
  43.7 1.7 %copy.5 = bf16[2,4,128,128]{3,2,1,0:T(8,128)(2,1)} copy(bf16[2,4,128,128]{3,2,1,0:T(8,128)(2,1)} %shard_map.37) | data formatting | bytes 524288

commit v3 on v2

--- a/solution.py
+++ b/solution.py
@@ -17,9 +17,10 @@
 NX = 4
 CH = 4
 BINS = 2048
-TILE = 128
+TILE = 256
 TILES = BINS // TILE
 PEERS = 2 * NY
+OWNERS = 4
 MESH = pl.DeviceIdType.MESH
 
 
@@ -36,7 +37,7 @@
 def kernel(
     spectra_ref, counts_hbm, table_ref, out_ref,
     raw, counts, white, wide_f32, left, left_wide, right, partner, table, pieces, landed, result,
-    local_sem, late_sem, left_send, left_recv, right_recv, import_send, along_send, mate_send,
+    local_sem, reply_sem, left_send, left_recv, right_recv, ahead_send, mate_send,
     out_send, out_recv,
 ):
     g = lax.axis_index("grp")
@@ -47,7 +48,6 @@
     x = (g // 2) % NX
     parity = z % 2
     q = z // 2
-    late = q >= 2
     me = parity * NY + y
     mate_g = g + 1 - 2 * core
 
@@ -64,32 +64,33 @@
     def row(other_q, group):
         return (group, (parity + 2 * other_q) * NY + y)
 
-    beside = q + 1 - 2 * (q % 2)
-    far = [(q + 2) % 4, (beside + 2) % 4]
     mate = (mate_g, d)
-    mirrored = z * NY + (NY - 1 - y)
-    import_to = ((g + 2) % NG, jnp.where(x == NX - 1, mirrored, d))
-    import_from = ((g - 2 + NG) % NG, jnp.where(x == 0, mirrored, d))
+    column_to = jnp.where(x == NX - 1, NY - 1 - y, y)
+    column_from = jnp.where(x == 0, NY - 1 - y, y)
+
+    def ahead(other_q):
+        return ((g + 2) % NG, (parity + 2 * other_q) * NY + column_to)
+
+    def behind(other_q):
+        return ((g - 2 + NG) % NG, (parity + 2 * other_q) * NY + column_from)
 
     barrier = pltpu.get_barrier_semaphore()
 
     def greet(device, semaphore=barrier):
         pl.semaphore_signal(semaphore, inc=1, device_id=device, device_id_type=MESH)
 
-    @pl.when(jnp.logical_not(late))
-    def _():
-        for other in far:
-            greet(row(other, g))
+    for other in range(1, 4):
+
+        @pl.when(other > q)
+        def _():
+            greet(behind(other))
+            greet(ahead(other))
             greet(row(other, mate_g))
 
-    greet(import_from)
+    greet(behind(q))
+    greet(mate)
     for step in range(1, PEERS):
         greet(peer((me + step) % PEERS))
-    greet(mate)
-    greet(row(beside, g))
-    greet(row(beside, mate_g))
-
-    near = 1 + (PEERS - 1) + 1 + 2
 
     load_counts.wait()
     load_raw.wait()
@@ -97,36 +98,30 @@
     for ch in range(CH):
         for s in range(2):
             values = raw[ch, s]
-            energy = jnp.sum(values * values) * (1.0 / (2 * BINS))
+            square = values * values
+            lanes = square[:, 0:128]
+            for t in range(1, BINS // 128):
+                lanes = lanes + square[:, t * 128 : (t + 1) * 128]
+            total = jnp.sum(jnp.sum(lanes, axis=0, keepdims=True), axis=1, keepdims=True)
             live = jnp.where(counts[s, block] > ch, 1.0, 0.0).astype(jnp.float32)
-            scale = live / jnp.sqrt(jnp.full((1, BINS), energy + 1e-06, jnp.float32))
+            scale = live / jnp.sqrt(total * (1.0 / (2 * BINS)) + 1e-06)
             wide_f32[s * 8 + ch : s * 8 + ch + 1, :] = values[0:1] * scale
             wide_f32[s * 8 + 4 + ch : s * 8 + 4 + ch + 1, :] = values[1:2] * scale
     white[...] = wide_f32[...].astype(jnp.bfloat16)
 
-    @pl.when(jnp.logical_not(late))
-    def _():
-        pl.semaphore_wait(barrier, near)
-
-    @pl.when(late)
-    def _():
-        pl.semaphore_wait(barrier, near + 4)
-        for other in far:
-            greet(row(other, g), late_sem)
-            greet(row(other, mate_g), late_sem)
-
-    def import_copy():
+    pl.semaphore_wait(barrier, PEERS + 1 + 3 * q)
+    for other in range(3):
+
+        @pl.when(other < q)
+        def _():
+            greet(behind(other), reply_sem.at[q])
+            greet(row(other, mate_g), reply_sem.at[q])
+
+    def ahead_copy(n, other):
         return pltpu.make_async_remote_copy(
             src_ref=white, dst_ref=right.at[1, q],
-            send_sem=import_send, recv_sem=right_recv.at[1, q],
-            device_id=import_to, device_id_type=MESH,
-        )
-
-    def along_copy(n, other):
-        return pltpu.make_async_remote_copy(
-            src_ref=right.at[1, q], dst_ref=right.at[1, q],
-            send_sem=along_send.at[n], recv_sem=right_recv.at[1, q],
-            device_id=row(other, g), device_id_type=MESH,
+            send_sem=ahead_send.at[n], recv_sem=right_recv.at[1, q],
+            device_id=ahead(other), device_id_type=MESH,
         )
 
     def own_copy(n, other):
@@ -146,70 +141,64 @@
     def arrival(k, other):
         return pltpu.make_async_remote_copy(
             src_ref=white, dst_ref=right.at[k, other],
-            send_sem=import_send, recv_sem=right_recv.at[k, other],
+            send_sem=ahead_send.at[0], recv_sem=right_recv.at[k, other],
             device_id=mate, device_id_type=MESH,
         )
 
-    def left_copy(n, slot):
-        return pltpu.make_async_remote_copy(
-            src_ref=white, dst_ref=left.at[me],
-            send_sem=left_send.at[n], recv_sem=left_recv.at[me],
-            device_id=peer(slot), device_id_type=MESH,
-        )
+    facing = (PEERS // 2 + me) % PEERS
+
+    def left_copy(source, slot, target, n):
+        return pltpu.make_async_remote_copy(
+            src_ref=source, dst_ref=left.at[slot],
+            send_sem=left_send.at[n], recv_sem=left_recv.at[slot],
+            device_id=peer(target), device_id_type=MESH,
+        )
+
+    def in_row(n):
+        return parity * NY + (y + n) % NY
+
+    def send_row(other):
+        ahead_copy(other, other).start()
+
+        @pl.when(core == 0)
+        def _():
+            own_copy(other, other).start()
+
+    for other in range(3):
+
+        @pl.when(other < q)
+        def _():
+            send_row(other)
+
+    for n in range(1, NY):
+        left_copy(white, me, in_row(n), n).start()
+    left_copy(white, me, facing, 0).start()
+    send_row(q)
 
     def left_arrival(slot):
-        return pltpu.make_async_remote_copy(
-            src_ref=white, dst_ref=left.at[slot],
-            send_sem=left_send.at[0], recv_sem=left_recv.at[slot],
-            device_id=peer(slot), device_id_type=MESH,
-        )
-
-    import_copy().start()
-
-    @pl.when(jnp.logical_and(core == 0, late))
-    def _():
-        own_copy(2, far[0]).start()
-        own_copy(3, far[1]).start()
-
-    @pl.when(core == 0)
-    def _():
-        own_copy(0, q).start()
-        own_copy(1, beside).start()
-
-    for n in range(PEERS - 1):
-        left_copy(n, (me + 1 + n) % PEERS).start()
-
-    arrival(1, q).wait_recv()
-
-    @pl.when(late)
-    def _():
-        along_copy(1, far[0]).start()
-        along_copy(2, far[1]).start()
-
-    along_copy(0, beside).start()
-
-    @pl.when(core == 1)
-    def _():
-        mate_copy(0, q).start()
-
-    @pl.when(jnp.logical_not(late))
-    def _():
-        pl.semaphore_wait(late_sem, 4)
-
-        @pl.when(core == 0)
-        def _():
-            own_copy(2, far[0]).start()
-            own_copy(3, far[1]).start()
-
-        along_copy(1, far[0]).start()
-        along_copy(2, far[1]).start()
+        left_copy(white, slot, facing, 0).wait_recv()
+
+    for n in range(1, NY):
+        left_arrival(in_row(n))
+        left_copy(left.at[in_row(n)], in_row(n), facing, NY - 1 + n).start()
+
+    for other in range(1, 4):
+
+        @pl.when(other > q)
+        def _():
+            pl.semaphore_wait(reply_sem.at[other], 2)
+            send_row(other)
 
     def widen(n, carry):
-        slot = (me + n) % PEERS
+        row_first = jnp.where(n < NY, parity, 1 - parity) * NY
+        slot = row_first + (y + n) % NY
+
+        @pl.when(n >= NY)
+        def _():
+            left_arrival(slot)
 
         @pl.when(n > 0)
         def _():
-            left_arrival(slot).wait_recv()
             wide_f32[...] = left[slot].astype(jnp.float32)
 
         def tile(t, inner):
@@ -244,17 +233,16 @@
             device_id=peer(slot), device_id_type=MESH,
         )
 
-    def half(e, carry):
+    def half(turn, carry):
+        e = (q // 2 + turn) % 2
         for zz in range(2):
             other = 2 * e + zz
 
-            @pl.when(other != q)
+            arrival(1, other).wait_recv()
+
+            @pl.when(core == 1)
             def _():
-                arrival(1, other).wait_recv()
-
-                @pl.when(core == 1)
-                def _():
-                    mate_copy((other - q + 4) % 4, other).start()
+                mate_copy(other, other).start()
 
         for zz in range(2):
             arrival(0, 2 * e + zz).wait_recv()
@@ -284,7 +272,8 @@
         both = jnp.where(row_id % 4 < limit, 0.5, 0.0).astype(jnp.float32)
 
         def owners(n, inner):
-            slots = [(me + 1 + 2 * n + i) % PEERS for i in range(2)]
+            pair = (y // 2 + 1 + n) % 2
+            slots = [(i // 2) * NY + pair * 2 + i % 2 for i in range(OWNERS)]
 
             def tile(t, acc):
                 columns = pl.ds(pl.multiple_of(t * TILE, TILE), TILE)
@@ -306,7 +295,7 @@
                 )
 
             lagged = lax.fori_loop(
-                0, TILES, tile, jnp.zeros((2 * CH * 16, LAGS), jnp.float32), unroll=2
+                0, TILES, tile, jnp.zeros((OWNERS * CH * 16, LAGS), jnp.float32), unroll=TILES
             )
             for i, slot in enumerate(slots):
                 at = g * (NZ * NY) + (2 * q + slot // NY) * NY + slot % NY
@@ -317,27 +306,28 @@
                     pieces[e, slot, ch] = (
                         lagged[first : first + 16] * (1.0 - both * factor)
                     ).astype(jnp.bfloat16)
-            out_copy(e, 2 * n, slots[0]).start()
-
-            @pl.when(n < PEERS // 2 - 1)
-            def _():
-                out_copy(e, 2 * n + 1, slots[1]).start()
+            for i, slot in enumerate(slots):
+
+                @pl.when(slot != me)
+                def _():
+                    out_copy(e, slot, slot).start()
 
             return inner
 
-        lax.fori_loop(0, PEERS // 2, owners, 0)
+        lax.fori_loop(0, PEERS // OWNERS, owners, 0)
         return carry
 
     lax.fori_loop(0, 2, half, 0)
 
     def store(e):
         return pltpu.make_async_copy(
-            result.at[:, :, pl.ds(e * 64, 64), :],
-            out_ref.at[:, :, pl.ds(e * 64, 64), :],
+            result.at[:, :, pl.ds(pl.multiple_of(e * 64, 64), 64), :],
+            out_ref.at[:, :, pl.ds(pl.multiple_of(e * 64, 64), 64), :],
             local_sem.at[3 + e],
         )
 
-    for e in range(2):
+    for turn in range(2):
+        e = (q // 2 + turn) % 2
         for n in range(PEERS - 1):
             out_arrival(e, (me + 1 + n) % PEERS).wait_recv()
         landed[e, me] = pieces[e, me]
@@ -360,26 +350,20 @@
         lax.fori_loop(0, 2 * CH, assemble, 0)
         store(e).start()
 
-    import_copy().wait_send()
     for n in range(PEERS - 1):
-        left_copy(n, (me + 1 + n) % PEERS).wait_send()
+        left_copy(white, me, facing, n).wait_send()
         for e in range(2):
-            out_copy(e, n, (me + 1 + n) % PEERS).wait_send()
-    along_copy(0, beside).wait_send()
-    along_copy(1, far[0]).wait_send()
-    along_copy(2, far[1]).wait_send()
-
-    @pl.when(core == 0)
-    def _():
-        own_copy(0, q).wait_send()
-        own_copy(1, beside).wait_send()
-        own_copy(2, far[0]).wait_send()
-        own_copy(3, far[1]).wait_send()
-
-    @pl.when(core == 1)
-    def _():
-        for n in range(4):
-            mate_copy(n, (q + n) % 4).wait_send()
+            out_copy(e, (me + 1 + n) % PEERS, facing).wait_send()
+    for other in range(4):
+        ahead_copy(other, other).wait_send()
+
+        @pl.when(core == 0)
+        def _():
+            own_copy(other, other).wait_send()
+
+        @pl.when(core == 1)
+        def _():
+            mate_copy(other, other).wait_send()
 
     store(0).wait()
     store(1).wait()
@@ -407,14 +391,13 @@
             pltpu.VMEM((2, PEERS, CH, 16, LAGS), bf16),
             pltpu.VMEM((ROUNDS, CH, NZ * NY * CH, LAGS), bf16),
             dma((5,)),
-            pltpu.SemaphoreType.REGULAR,
+            pltpu.SemaphoreType.REGULAR((4,)),
             dma((PEERS - 1,)),
             dma((PEERS,)),
             dma((ROUNDS, 4)),
-            dma,
-            dma((3,)),
             dma((4,)),
-            dma((2, PEERS - 1)),
+            dma((4,)),
+            dma((2, PEERS)),
             dma((2, PEERS)),
         ],
         compiler_params=pltpu.CompilerParams(

time: 45.6 us -> 39.9 us (0.87)
  the two profiles are of different devices: /device:TPU:8 before, /device:TPU:6 now
where the time goes in v3:
time: 39.9 us; the launch traced here: 39.8 us
  Pallas kernels  38.1 us (95%)
  local copies, waits for them, and re-layouts  1.67 us (4%)
    pallas_call x1, Pallas kernels, local(): pl.pallas_call(kernel, out_shape=jax.ShapeDtypeStruct((ROUNDS, CH, NZ * N...  38.1 us
    unnamed x1, local copies, waits for them, and re-layouts  1.67 us

profile of v3, /device:TPU:6, one launch (start us, length us, event | category | flops | bytes accessed | tf_op | source)
XLA Modules:
  0.0 39.8 jit_solution(3922193057518948509)
XLA Ops:
  0.0 38.1 %shard_map.37 = bf16[2,4,128,128]{3,2,1,0:T(8,128)(2,1)} custom-call(f32[4,2,2,2048]{3,2,1,0:T(2,128)} %spectra_ref.1, s32[2,512]{1,0:T(2,128)} %counts_hbm.1, bf16[4096,128]{1,0:T(8,128)(2,1)} %constant.2.clone.table_ref), custom_call_target="tpu_custom_call" | custom-call | flops 1100000000 | bytes 1600000 | tf_op jit(solution)/shard_map/pallas_call | solution.py:375
  38.1 1.7 %copy.5 = bf16[2,4,128,128]{3,2,1,0:T(8,128)(2,1)} copy(bf16[2,4,128,128]{3,2,1,0:T(8,128)(2,1)} %shard_map.37) | data formatting | bytes 524288

commit v4 on v3

--- a/solution.py
+++ b/solution.py
@@ -17,7 +17,7 @@
 NX = 4
 CH = 4
 BINS = 2048
-TILE = 256
+TILE = 512
 TILES = BINS // TILE
 PEERS = 2 * NY
 OWNERS = 4
@@ -36,8 +36,8 @@
 
 def kernel(
     spectra_ref, counts_hbm, table_ref, out_ref,
-    raw, counts, white, wide_f32, left, left_wide, right, partner, table, pieces, landed, result,
-    local_sem, reply_sem, left_send, left_recv, right_recv, ahead_send, mate_send,
+    raw, counts, white, fed, wide_f32, left, left_wide, right, partner, table, pieces, landed, result,
+    local_sem, reply_sem, left_send, left_recv, right_recv, ahead_send, feed_sem, spread_send, mate_send,
     out_send, out_recv,
 ):
     g = lax.axis_index("grp")
@@ -64,6 +64,8 @@
     def row(other_q, group):
         return (group, (parity + 2 * other_q) * NY + y)
 
+    late = q >= 2
+    beside = q + 1 - 2 * (q % 2)
     mate = (mate_g, d)
     column_to = jnp.where(x == NX - 1, NY - 1 - y, y)
     column_from = jnp.where(x == 0, NY - 1 - y, y)
@@ -71,26 +73,42 @@
     def ahead(other_q):
         return ((g + 2) % NG, (parity + 2 * other_q) * NY + column_to)
 
+    feeds = jnp.logical_and(x == NX - 1, core == 0)
+    spreads = jnp.logical_and(x == 0, core == 0)
+    fed_by = ((g + 6) % NG, d)
+    feed_to = ((g + 10) % NG, d)
+
     def behind(other_q):
-        return ((g - 2 + NG) % NG, (parity + 2 * other_q) * NY + column_from)
+        group = jnp.where(spreads, g + 8, g - 2 + NG) % NG
+        return (group, (parity + 2 * other_q) * NY + column_from)
 
     barrier = pltpu.get_barrier_semaphore()
 
     def greet(device, semaphore=barrier):
         pl.semaphore_signal(semaphore, inc=1, device_id=device, device_id_type=MESH)
 
-    for other in range(1, 4):
-
-        @pl.when(other > q)
-        def _():
+    @pl.when(jnp.logical_not(late))
+    def _():
+        for other in (2, 3):
             greet(behind(other))
-            greet(ahead(other))
             greet(row(other, mate_g))
 
+        @pl.when(jnp.logical_not(feeds))
+        def _():
+            for other in (2, 3):
+                greet(ahead(other))
+
+    @pl.when(spreads)
+    def _():
+        greet(fed_by)
+
     greet(behind(q))
+    greet(behind(beside))
     greet(mate)
+    greet(row(beside, mate_g))
     for step in range(1, PEERS):
         greet(peer((me + step) % PEERS))
+    near = 4 + PEERS - 1 + jnp.where(spreads, 2, 0) - jnp.where(feeds, 1, 0)
 
     load_counts.wait()
     load_raw.wait()
@@ -109,11 +127,14 @@
             wide_f32[s * 8 + 4 + ch : s * 8 + 4 + ch + 1, :] = values[1:2] * scale
     white[...] = wide_f32[...].astype(jnp.bfloat16)
 
-    pl.semaphore_wait(barrier, PEERS + 1 + 3 * q)
-    for other in range(3):
-
-        @pl.when(other < q)
-        def _():
+    @pl.when(jnp.logical_not(late))
+    def _():
+        pl.semaphore_wait(barrier, near)
+
+    @pl.when(late)
+    def _():
+        pl.semaphore_wait(barrier, near + 6 - jnp.where(feeds, 2, 0))
+        for other in (0, 1):
             greet(behind(other), reply_sem.at[q])
             greet(row(other, mate_g), reply_sem.at[q])
 
@@ -155,39 +176,83 @@
         )
 
     def in_row(n):
-        return parity * NY + (y + n) % NY
+        flipped = y + 1 - 2 * (y % 2)
+        return parity * NY + (flipped if n == 1 else (y + 2) % NY if n == 2 else (flipped + 2) % NY)
+
+    def feed_copy():
+        return pltpu.make_async_remote_copy(
+            src_ref=white, dst_ref=fed, send_sem=feed_sem.at[0], recv_sem=feed_sem.at[1],
+            device_id=feed_to, device_id_type=MESH,
+        )
+
+    def spread_copy(other):
+        return pltpu.make_async_remote_copy(
+            src_ref=fed, dst_ref=right.at[1, q],
+            send_sem=spread_send.at[other], recv_sem=right_recv.at[1, q],
+            device_id=behind(other), device_id_type=MESH,
+        )
 
     def send_row(other):
-        ahead_copy(other, other).start()
+        @pl.when(jnp.logical_not(feeds))
+        def _():
+            ahead_copy(other, other).start()
 
         @pl.when(core == 0)
         def _():
             own_copy(other, other).start()
 
-    for other in range(3):
-
-        @pl.when(other < q)
-        def _():
+    @pl.when(feeds)
+    def _():
+        feed_copy().start()
+
+    @pl.when(late)
+    def _():
+        for other in (0, 1):
             send_row(other)
 
+    send_row(q)
+    send_row(beside)
     for n in range(1, NY):
         left_copy(white, me, in_row(n), n).start()
     left_copy(white, me, facing, 0).start()
-    send_row(q)
 
     def left_arrival(slot):
         left_copy(white, slot, facing, 0).wait_recv()
+
+    @pl.when(spreads)
+    def _():
+        feed_copy().wait_recv()
+
+        @pl.when(late)
+        def _():
+            spread_copy(0).start()
+            spread_copy(1).start()
+
+        spread_copy(q).start()
+        spread_copy(beside).start()
 
     for n in range(1, NY):
         left_arrival(in_row(n))
         left_copy(left.at[in_row(n)], in_row(n), facing, NY - 1 + n).start()
 
-    for other in range(1, 4):
-
-        @pl.when(other > q)
-        def _():
-            pl.semaphore_wait(reply_sem.at[other], 2)
+    for other in (q, beside):
+        arrival(1, other).wait_recv()
+
+        @pl.when(core == 1)
+        def _():
+            mate_copy(other, other).start()
+
+    @pl.when(jnp.logical_not(late))
+    def _():
+        for other in (2, 3):
+            pl.semaphore_wait(
+                reply_sem.at[other], 2 + jnp.where(spreads, 1, 0) - jnp.where(feeds, 1, 0)
+            )
             send_row(other)
+
+            @pl.when(spreads)
+            def _():
+                spread_copy(other).start()
 
     def widen(n, carry):
         row_first = jnp.where(n < NY, parity, 1 - parity) * NY
@@ -235,14 +300,14 @@
 
     def half(turn, carry):
         e = (q // 2 + turn) % 2
-        for zz in range(2):
-            other = 2 * e + zz
-
-            arrival(1, other).wait_recv()
-
-            @pl.when(core == 1)
-            def _():
-                mate_copy(other, other).start()
+        @pl.when(turn == 1)
+        def _():
+            for zz in range(2):
+                arrival(1, 2 * e + zz).wait_recv()
+
+                @pl.when(core == 1)
+                def _():
+                    mate_copy(2 * e + zz, 2 * e + zz).start()
 
         for zz in range(2):
             arrival(0, 2 * e + zz).wait_recv()
@@ -295,7 +360,7 @@
                 )
 
             lagged = lax.fori_loop(
-                0, TILES, tile, jnp.zeros((OWNERS * CH * 16, LAGS), jnp.float32), unroll=TILES
+                0, TILES, tile, jnp.zeros((OWNERS * CH * 16, LAGS), jnp.float32), unroll=2
             )
             for i, slot in enumerate(slots):
                 at = g * (NZ * NY) + (2 * q + slot // NY) * NY + slot % NY
@@ -354,8 +419,19 @@
         left_copy(white, me, facing, n).wait_send()
         for e in range(2):
             out_copy(e, (me + 1 + n) % PEERS, facing).wait_send()
+    @pl.when(feeds)
+    def _():
+        feed_copy().wait_send()
+
     for other in range(4):
-        ahead_copy(other, other).wait_send()
+
+        @pl.when(jnp.logical_not(feeds))
+        def _():
+            ahead_copy(other, other).wait_send()
+
+        @pl.when(spreads)
+        def _():
+            spread_copy(other).wait_send()
 
         @pl.when(core == 0)
         def _():
@@ -380,6 +456,7 @@
         scratch_shapes=[
             pltpu.VMEM((CH, 2, 2, BINS), jnp.float32),
             pltpu.SMEM(counts.shape, jnp.int32),
+            pltpu.VMEM((16, BINS), bf16),
             pltpu.VMEM((16, BINS), bf16),
             pltpu.VMEM((16, BINS), jnp.float32),
             pltpu.VMEM((PEERS, 16, BINS), bf16),
@@ -396,6 +473,8 @@
             dma((PEERS,)),
             dma((ROUNDS, 4)),
             dma((4,)),
+            dma((2,)),
+            dma((4,)),
             dma((4,)),
             dma((2, PEERS)),
             dma((2, PEERS)),

time: 39.9 us -> 38.7 us (0.970)
  the two profiles are of different devices: /device:TPU:6 before, /device:TPU:320 now
where the time goes in v4:
time: 38.7 us; the launch traced here: 38.6 us
  Pallas kernels  36.9 us (95%)
  local copies, waits for them, and re-layouts  1.67 us (4%)
    pallas_call x1, Pallas kernels, local(): pl.pallas_call(kernel, out_shape=jax.ShapeDtypeStruct((ROUNDS, CH, NZ * N...  36.9 us
    unnamed x1, local copies, waits for them, and re-layouts  1.67 us

profile of v4, /device:TPU:320, one launch (start us, length us, event | category | flops | bytes accessed | tf_op | source)
XLA Modules:
  0.0 38.6 jit_solution(12423294714977374591)
XLA Ops:
  0.0 36.9 %shard_map.37 = bf16[2,4,128,128]{3,2,1,0:T(8,128)(2,1)} custom-call(f32[4,2,2,2048]{3,2,1,0:T(2,128)} %spectra_ref.1, s32[2,512]{1,0:T(2,128)} %counts_hbm.1, bf16[4096,128]{1,0:T(8,128)(2,1)} %constant.2.clone.table_ref), custom_call_target="tpu_custom_call" | custom-call | flops 1100000000 | bytes 1600000 | tf_op jit(solution)/shard_map/pallas_call | solution.py:451
  36.9 1.7 %copy.5 = bf16[2,4,128,128]{3,2,1,0:T(8,128)(2,1)} copy(bf16[2,4,128,128]{3,2,1,0:T(8,128)(2,1)} %shard_map.37) | data formatting | bytes 524288

commit v5 on v4

--- a/solution.py
+++ b/solution.py
@@ -79,7 +79,8 @@
     feed_to = ((g + 10) % NG, d)
 
     def behind(other_q):
-        group = jnp.where(spreads, g + 8, g - 2 + NG) % NG
+        spread = jnp.logical_and(spreads, other_q // 2 != q // 2)
+        group = jnp.where(spread, g + 8, g - 2 + NG) % NG
         return (group, (parity + 2 * other_q) * NY + column_from)
 
     barrier = pltpu.get_barrier_semaphore()
@@ -108,7 +109,7 @@
     greet(row(beside, mate_g))
     for step in range(1, PEERS):
         greet(peer((me + step) % PEERS))
-    near = 4 + PEERS - 1 + jnp.where(spreads, 2, 0) - jnp.where(feeds, 1, 0)
+    near = 4 + PEERS - 1 + jnp.where(feeds, 1, 0)
 
     load_counts.wait()
     load_raw.wait()
@@ -192,8 +193,11 @@
             device_id=behind(other), device_id_type=MESH,
         )
 
+    def straight(other):
+        return jnp.logical_or(jnp.logical_not(feeds), other // 2 == q // 2)
+
     def send_row(other):
-        @pl.when(jnp.logical_not(feeds))
+        @pl.when(straight(other))
         def _():
             ahead_copy(other, other).start()
 
@@ -227,9 +231,6 @@
         def _():
             spread_copy(0).start()
             spread_copy(1).start()
-
-        spread_copy(q).start()
-        spread_copy(beside).start()
 
     for n in range(1, NY):
         left_arrival(in_row(n))
@@ -425,11 +426,11 @@
 
     for other in range(4):
 
-        @pl.when(jnp.logical_not(feeds))
+        @pl.when(straight(other))
         def _():
             ahead_copy(other, other).wait_send()
 
-        @pl.when(spreads)
+        @pl.when(jnp.logical_and(spreads, other // 2 != q // 2))
         def _():
             spread_copy(other).wait_send()
 

time: 38.7 us -> 37.6 us (0.972)
  the two profiles are of different devices: /device:TPU:320 before, /device:TPU:6 now
where the time goes in v5:
time: 37.6 us; the launch traced here: 37.4 us
  Pallas kernels  35.7 us (95%)
  local copies, waits for them, and re-layouts  1.67 us (4%)
    pallas_call x1, Pallas kernels, local(): pl.pallas_call(kernel, out_shape=jax.ShapeDtypeStruct((ROUNDS, CH, NZ * N...  35.7 us
    unnamed x1, local copies, waits for them, and re-layouts  1.67 us

profile of v5, /device:TPU:6, one launch (start us, length us, event | category | flops | bytes accessed | tf_op | source)
XLA Modules:
  0.0 37.4 jit_solution(12139743622026719167)
XLA Ops:
  0.0 35.7 %shard_map.37 = bf16[2,4,128,128]{3,2,1,0:T(8,128)(2,1)} custom-call(f32[4,2,2,2048]{3,2,1,0:T(2,128)} %spectra_ref.1, s32[2,512]{1,0:T(2,128)} %counts_hbm.1, bf16[4096,128]{1,0:T(8,128)(2,1)} %constant.2.clone.table_ref), custom_call_target="tpu_custom_call" | custom-call | flops 1100000000 | bytes 1600000 | tf_op jit(solution)/shard_map/pallas_call | solution.py:452
  35.8 1.7 %copy.5 = bf16[2,4,128,128]{3,2,1,0:T(8,128)(2,1)} copy(bf16[2,4,128,128]{3,2,1,0:T(8,128)(2,1)} %shard_map.37) | data formatting | bytes 524288

commit v6 on v5

--- a/solution.py
+++ b/solution.py
@@ -278,7 +278,7 @@
         lax.fori_loop(0, TILES, tile, 0)
         return carry
 
-    lax.fori_loop(0, PEERS, widen, 0)
+    lax.fori_loop(0, NY, widen, 0)
     load_table.wait()
 
     mirror = x == 0
@@ -338,8 +338,18 @@
         both = jnp.where(row_id % 4 < limit, 0.5, 0.0).astype(jnp.float32)
 
         def owners(n, inner):
+            first = turn == 0
             pair = (y // 2 + 1 + n) % 2
-            slots = [(i // 2) * NY + pair * 2 + i % 2 for i in range(OWNERS)]
+            side = (parity + n) % 2
+            slots = [
+                jnp.where(first, side * NY + i, (i // 2) * NY + pair * 2 + i % 2)
+                for i in range(OWNERS)
+            ]
+
+            @pl.when(jnp.logical_and(first, n == 1))
+            def _():
+                lax.fori_loop(NY, PEERS, widen, 0)
+
 
             def tile(t, acc):
                 columns = pl.ds(pl.multiple_of(t * TILE, TILE), TILE)
@@ -368,9 +378,9 @@
                 least = jnp.minimum(counts[0, at], counts[1, at])
                 for ch in range(CH):
                     factor = jnp.where(least > ch, 1.0, 0.0).astype(jnp.float32)
-                    first = (i * CH + ch) * 16
+                    at_row = (i * CH + ch) * 16
                     pieces[e, slot, ch] = (
-                        lagged[first : first + 16] * (1.0 - both * factor)
+                        lagged[at_row : at_row + 16] * (1.0 - both * factor)
                     ).astype(jnp.bfloat16)
             for i, slot in enumerate(slots):
 

time: 37.6 us -> 36.5 us (0.971)
  Pallas kernels: 35.7 us -> 34.6 us
    pallas_call x1, Pallas kernels: 35.7 us -> 34.6 us  [local(): pl.pallas_call(kernel, out_shape=jax.ShapeDtypeStruct((ROUNDS, CH, NZ * N...]
where the time goes in v6:
time: 36.5 us; the launch traced here: 36.3 us
  Pallas kernels  34.6 us (95%)
  local copies, waits for them, and re-layouts  1.67 us (5%)
    pallas_call x1, Pallas kernels, local(): pl.pallas_call(kernel, out_shape=jax.ShapeDtypeStruct((ROUNDS, CH, NZ * N...  34.6 us
    unnamed x1, local copies, waits for them, and re-layouts  1.67 us

profile of v6, /device:TPU:6, one launch (start us, length us, event | category | flops | bytes accessed | tf_op | source)
XLA Modules:
  0.0 36.3 jit_solution(1726969613235050447)
XLA Ops:
  0.0 34.6 %shard_map.37 = bf16[2,4,128,128]{3,2,1,0:T(8,128)(2,1)} custom-call(f32[4,2,2,2048]{3,2,1,0:T(2,128)} %spectra_ref.1, s32[2,512]{1,0:T(2,128)} %counts_hbm.1, bf16[4096,128]{1,0:T(8,128)(2,1)} %constant.2.clone.table_ref), custom_call_target="tpu_custom_call" | custom-call | flops 1100000000 | bytes 1600000 | tf_op jit(solution)/shard_map/pallas_call | solution.py:462
  34.7 1.7 %copy.5 = bf16[2,4,128,128]{3,2,1,0:T(8,128)(2,1)} copy(bf16[2,4,128,128]{3,2,1,0:T(8,128)(2,1)} %shard_map.37) | data formatting | bytes 524288

commit v7 on v6

--- a/solution.py
+++ b/solution.py
@@ -223,28 +223,22 @@
     def left_arrival(slot):
         left_copy(white, slot, facing, 0).wait_recv()
 
-    @pl.when(spreads)
+    @pl.when(jnp.logical_and(spreads, late))
     def _():
         feed_copy().wait_recv()
-
-        @pl.when(late)
-        def _():
-            spread_copy(0).start()
-            spread_copy(1).start()
+        spread_copy(0).start()
+        spread_copy(1).start()
 
     for n in range(1, NY):
         left_arrival(in_row(n))
         left_copy(left.at[in_row(n)], in_row(n), facing, NY - 1 + n).start()
 
-    for other in (q, beside):
-        arrival(1, other).wait_recv()
-
-        @pl.when(core == 1)
-        def _():
-            mate_copy(other, other).start()
-
     @pl.when(jnp.logical_not(late))
     def _():
+        @pl.when(spreads)
+        def _():
+            feed_copy().wait_recv()
+
         for other in (2, 3):
             pl.semaphore_wait(
                 reply_sem.at[other], 2 + jnp.where(spreads, 1, 0) - jnp.where(feeds, 1, 0)
@@ -254,6 +248,13 @@
             @pl.when(spreads)
             def _():
                 spread_copy(other).start()
+
+    for other in (q, beside):
+        arrival(1, other).wait_recv()
+
+        @pl.when(core == 1)
+        def _():
+            mate_copy(other, other).start()
 
     def widen(n, carry):
         row_first = jnp.where(n < NY, parity, 1 - parity) * NY

time: 36.5 us -> 36.5 us (level)
  no operation moved by 1% of the time
where the time goes in v7:
time: 36.5 us; the launch traced here: 36.3 us
  Pallas kernels  34.7 us (95%)
  local copies, waits for them, and re-layouts  1.67 us (5%)
    pallas_call x1, Pallas kernels, local(): pl.pallas_call(kernel, out_shape=jax.ShapeDtypeStruct((ROUNDS, CH, NZ * N...  34.7 us
    unnamed x1, local copies, waits for them, and re-layouts  1.67 us

profile of v7, /device:TPU:6, one launch (start us, length us, event | category | flops | bytes accessed | tf_op | source)
XLA Modules:
  0.0 36.3 jit_solution(7063170802362724808)
XLA Ops:
  0.0 34.7 %shard_map.37 = bf16[2,4,128,128]{3,2,1,0:T(8,128)(2,1)} custom-call(f32[4,2,2,2048]{3,2,1,0:T(2,128)} %spectra_ref.1, s32[2,512]{1,0:T(2,128)} %counts_hbm.1, bf16[4096,128]{1,0:T(8,128)(2,1)} %constant.2.clone.table_ref), custom_call_target="tpu_custom_call" | custom-call | flops 1100000000 | bytes 1600000 | tf_op jit(solution)/shard_map/pallas_call | solution.py:463
  34.7 1.7 %copy.5 = bf16[2,4,128,128]{3,2,1,0:T(8,128)(2,1)} copy(bf16[2,4,128,128]{3,2,1,0:T(8,128)(2,1)} %shard_map.37) | data formatting | bytes 524288

commit v8 on v7

--- a/solution.py
+++ b/solution.py
@@ -214,11 +214,11 @@
         for other in (0, 1):
             send_row(other)
 
-    send_row(q)
-    send_row(beside)
     for n in range(1, NY):
         left_copy(white, me, in_row(n), n).start()
     left_copy(white, me, facing, 0).start()
+    send_row(q)
+    send_row(beside)
 
     def left_arrival(slot):
         left_copy(white, slot, facing, 0).wait_recv()

time: 36.5 us -> 35.8 us (0.981); the launches traced: 36.3 us -> 35.2 us
  Pallas kernels: 34.7 us -> 33.6 us
    pallas_call x1, Pallas kernels: 34.7 us -> 33.6 us  [local(): pl.pallas_call(kernel, out_shape=jax.ShapeDtypeStruct((ROUNDS, CH, NZ * N...]
where the time goes in v8:
time: 35.8 us; the launch traced here: 35.2 us
  Pallas kernels  33.6 us (94%)
  local copies, waits for them, and re-layouts  1.67 us (5%)
    pallas_call x1, Pallas kernels, local(): pl.pallas_call(kernel, out_shape=jax.ShapeDtypeStruct((ROUNDS, CH, NZ * N...  33.6 us
    unnamed x1, local copies, waits for them, and re-layouts  1.67 us

profile of v8, /device:TPU:6, one launch (start us, length us, event | category | flops | bytes accessed | tf_op | source)
XLA Modules:
  0.0 35.2 jit_solution(11521531896285640674)
XLA Ops:
  0.0 33.6 %shard_map.37 = bf16[2,4,128,128]{3,2,1,0:T(8,128)(2,1)} custom-call(f32[4,2,2,2048]{3,2,1,0:T(2,128)} %spectra_ref.1, s32[2,512]{1,0:T(2,128)} %counts_hbm.1, bf16[4096,128]{1,0:T(8,128)(2,1)} %constant.2.clone.table_ref), custom_call_target="tpu_custom_call" | custom-call | flops 1100000000 | bytes 1600000 | tf_op jit(solution)/shard_map/pallas_call | solution.py:463
  33.6 1.7 %copy.5 = bf16[2,4,128,128]{3,2,1,0:T(8,128)(2,1)} copy(bf16[2,4,128,128]{3,2,1,0:T(8,128)(2,1)} %shard_map.37) | data formatting | bytes 524288
